TPU v7x, 256 devices: a whole 4x4x8 slice. The times are simulated.
256 devices in a mesh: segment: 8 (over z_lo, x), rep: 32 (over y, z_hi, core).
Axes of the slice: x: 4, y: 4, z: 8 (z_hi: 4, z_lo: 2; z = z_hi * 2 + z_lo), core: 2. Of those that a mesh axis runs over, the one named last changes fastest.
Arguments:
- feature_maps: bfloat16 [2048, 7, 7, 1024], P(('segment', 'rep')), may hold values from -6 to 6
- path_lists: int32 [1, 2048, 1], P(None, ('segment', 'rep')), may hold values from 0 to 7; in each aligned block of 8 rows (0 to 7, 8 to 15, ..., all dimensions but the last counted through in order) at most 2 rows name the same one
- point_weight: bfloat16 [1, 8, 1024, 1024], P(None, 'segment'), may hold values from -0.1875 to 0.1875
- depth_kernel: float32 [1, 8, 25, 1024], P(None, 'segment'), may hold values from -1.8 to 1.8
- cotangent: bfloat16 [2048, 7, 7, 1024], P(('segment', 'rep')), may hold values from -6 to 6
Outputs:
- final_maps: bfloat16 [2048, 7, 7, 1024], P(('segment', 'rep'))
- input_grad: bfloat16 [2048, 7, 7, 1024], P(('segment', 'rep'))
- point_grad: float32 [1, 8, 1024, 1024], P(None, 'segment', 'rep')
- depth_grad: float32 [1, 8, 25, 1024], P(None, 'segment')
Inputs may be any that keep to these rules, and one draw needn't show every extreme that they name: `path_lists`: in each layer, among the 8 samples of one device no operator is chosen by more than 2 samples.
All inputs are finite; a program needn't handle non-finite values.
Results may differ from a plain program's by a relative error of at most 0.0032.
Values may be sent and summed in bfloat16 or wider, within the bound.
A program may use at most 128 MiB of HBM per device.

v0:
```python
import jax
import jax.numpy as jnp
from jax import lax
from jax.sharding import PartitionSpec as P

LAYERS = 1


EPS = 1e-05


def tap_mask(op_kind):
    tap_index = jnp.arange(25, dtype=jnp.int32)
    row_shift = tap_index // 5 - 2
    col_shift = tap_index % 5 - 2
    narrow = (jnp.abs(row_shift) <= 1) & (jnp.abs(col_shift) <= 1)
    spaced = (row_shift % 2 == 0) & (col_shift % 2 == 0)
    tap_keep = jnp.where(op_kind == 0, narrow, jnp.where(op_kind == 1, True, spaced))
    return tap_keep.astype(jnp.float32)


def shift_window(padded, row_shift, col_shift, map_side):
    return padded[
        :, 2 + row_shift : 2 + row_shift + map_side, 2 + col_shift : 2 + col_shift + map_side, :
    ]


def depthwise(source, kernel):
    map_side = source.shape[1]
    padded = jnp.pad(source, ((0, 0), (2, 2), (2, 2), (0, 0)))
    summed = jnp.zeros_like(source)
    for offset in range(25):
        summed = summed + kernel[offset] * shift_window(
            padded, offset // 5 - 2, offset % 5 - 2, map_side
        )
    return summed


def depthwise_back(grad_maps, kernel):
    map_side = grad_maps.shape[1]
    padded = jnp.pad(grad_maps, ((0, 0), (2, 2), (2, 2), (0, 0)))
    summed = jnp.zeros_like(grad_maps)
    for offset in range(25):
        summed = summed + kernel[offset] * shift_window(
            padded, 2 - offset // 5, 2 - offset % 5, map_side
        )
    return summed


def kernel_grad(grad_maps, source):
    map_side = source.shape[1]
    padded = jnp.pad(source, ((0, 0), (2, 2), (2, 2), (0, 0)))
    tap_rows = [
        jnp.sum(
            grad_maps * shift_window(padded, offset // 5 - 2, offset % 5 - 2, map_side),
            axis=(0, 1, 2),
        )
        for offset in range(25)
    ]
    return jnp.stack(tap_rows)


def block_forward(inputs, pointwise, kernel):
    channels = inputs.shape[-1]
    source = inputs.astype(jnp.float32)
    mixed_taps = depthwise(source, kernel)
    scaled = mixed_taps * lax.rsqrt(jnp.mean(mixed_taps * mixed_taps, axis=-1, keepdims=True) + EPS)
    active = (scaled * jax.nn.sigmoid(scaled)).astype(jnp.bfloat16)
    branch = jnp.dot(active.reshape(-1, channels), pointwise, preferred_element_type=jnp.float32)
    return (source + branch.reshape(source.shape)).astype(jnp.bfloat16)


def block_backward(inputs, grad_maps, pointwise, kernel):
    channels = inputs.shape[-1]
    source = inputs.astype(jnp.float32)
    mixed_taps = depthwise(source, kernel)
    inverse = lax.rsqrt(jnp.mean(mixed_taps * mixed_taps, axis=-1, keepdims=True) + EPS)
    scaled = mixed_taps * inverse
    logistic = jax.nn.sigmoid(scaled)
    active = (scaled * logistic).astype(jnp.bfloat16)
    flat_grads = grad_maps.reshape(-1, channels)
    back_act = lax.dot_general(
        flat_grads, pointwise, (((1,), (1,)), ((), ())), preferred_element_type=jnp.float32
    ).reshape(source.shape)
    grad_scaled = back_act * logistic * (1.0 + scaled * (1.0 - logistic))
    grad_mixed = inverse * (
        grad_scaled - scaled * jnp.mean(grad_scaled * scaled, axis=-1, keepdims=True)
    )
    grad_in = (grad_maps.astype(jnp.float32) + depthwise_back(grad_mixed, kernel)).astype(
        jnp.bfloat16
    )
    return (grad_in, active.reshape(-1, channels), flat_grads, kernel_grad(grad_mixed, source))


def point_term(active, flat_grads):
    return lax.dot_general(
        active, flat_grads, (((0,), (0,)), ((), ())), preferred_element_type=jnp.float32
    )


def dispatch_table(path_row, sections, capacity):
    samples = path_row.shape[0]
    earlier = (
        jnp.arange(samples, dtype=jnp.int32)[None, :]
        < jnp.arange(samples, dtype=jnp.int32)[:, None]
    )
    same_path = (path_row[None, :] == path_row[:, None]) & earlier
    path_rank = jnp.sum(same_path.astype(jnp.int32), axis=1)
    slot_of = path_row * capacity + path_rank
    return (jnp.arange(sections * capacity, dtype=jnp.int32)[:, None] == slot_of[None, :]).astype(
        jnp.bfloat16
    )


def apply_block(slot_items, pointwise, kernel):
    flat_rows = slot_items.reshape((-1,) + slot_items.shape[2:])
    return (block_forward(flat_rows, pointwise, kernel).reshape(slot_items.shape), slot_items)


def body(feature_maps, path_lists, point_weight, depth_kernel, cotangent):
    sections = lax.axis_size("segment")
    section = lax.axis_index("segment")
    samples_here = feature_maps.shape[0]
    capacity = max(max(2, samples_here // 4), (samples_here + sections - 1) // sections)
    tap_keep = tap_mask(section % 3)[:, None]
    map_side = feature_maps.shape[1]
    channels = feature_maps.shape[3]
    current = feature_maps
    layer_at = 0
    routing = dispatch_table(path_lists[layer_at, :, 0], sections, capacity)
    outgoing = jnp.einsum(
        "ks,shwc->khwc", routing, current, preferred_element_type=jnp.float32
    ).astype(jnp.bfloat16)
    outgoing = outgoing.reshape(sections, capacity, map_side, map_side, channels)
    kernel = depth_kernel[layer_at, 0] * tap_keep
    results, received = apply_block(
        lax.all_to_all(outgoing, "segment", split_axis=0, concat_axis=0, tiled=True),
        pointwise=point_weight[layer_at, 0],
        kernel=kernel,
    )
    returned = lax.all_to_all(results, "segment", split_axis=0, concat_axis=0, tiled=True)
    returned = returned.reshape(-1, map_side, map_side, channels)
    current = jnp.einsum(
        "ks,khwc->shwc", routing, returned, preferred_element_type=jnp.float32
    ).astype(jnp.bfloat16)
    tables = [routing]
    stored = [received.reshape(-1, map_side, map_side, channels)]
    grad_maps = cotangent
    point_parts = []
    depth_parts = []
    for layer_at in reversed(range(LAYERS)):
        routing = tables[layer_at]
        outgoing = jnp.einsum(
            "ks,shwc->khwc", routing, grad_maps, preferred_element_type=jnp.float32
        ).astype(jnp.bfloat16)
        outgoing = outgoing.reshape(sections, capacity, map_side, map_side, channels)
        arriving = lax.all_to_all(outgoing, "segment", split_axis=0, concat_axis=0, tiled=True)
        arriving = arriving.reshape(-1, map_side, map_side, channels)
        kernel = depth_kernel[layer_at, 0] * tap_keep
        grad_in, active, flat_grads, depth_term = block_backward(
            stored[layer_at], arriving, point_weight[layer_at, 0], kernel
        )
        depth_parts.append(depth_term * tap_keep)
        point_parts.append(point_term(active, flat_grads))
        sendback = lax.all_to_all(
            grad_in.reshape(sections, capacity, map_side, map_side, channels),
            "segment",
            split_axis=0,
            concat_axis=0,
            tiled=True,
        )
        sendback = sendback.reshape(-1, map_side, map_side, channels)
        grad_maps = jnp.einsum(
            "ks,khwc->shwc", routing, sendback, preferred_element_type=jnp.float32
        ).astype(jnp.bfloat16)
    point_parts = point_parts[::-1]
    depth_parts = depth_parts[::-1]
    point_grad = lax.psum_scatter(jnp.stack(point_parts), "rep", scatter_dimension=1, tiled=True)
    depth_grad = lax.psum(jnp.stack(depth_parts), "rep")
    return (current, grad_maps, point_grad[:, None], depth_grad[:, None])


def solution(mesh):
    placed = (
        P(("segment", "rep"), None, None, None),
        P(None, ("segment", "rep"), None),
        P(None, "segment", None, None),
        P(None, "segment", None, None),
        P(("segment", "rep"), None, None, None),
    )
    return jax.shard_map(
        body,
        mesh=mesh,
        in_specs=placed,
        out_specs=(
            P(("segment", "rep"), None, None, None),
            P(("segment", "rep"), None, None, None),
            P(None, "segment", "rep", None),
            P(None, "segment", None, None),
        ),
        check_vma=False,
    )
```

profile of v0, /device:TPU:1, one launch (start us, length us, event | category | flops | bytes accessed | tf_op | source)
XLA Modules:
  0.0 494.2 jit_solution(4348927070160416517)
XLA Ops:
  7.2 0.0 copy-start
  7.2 1.0 convert_reduce_fusion
  8.2 0.7 multiply_add_fusion.1
  8.8 3.0 convolution_convert_fusion
  11.8 4.5 reshape.517
  16.4 3.8 copy.47
  20.1 6.2 %all-to-all-start.2 = ((bf16[8,2,7,7,1024]{4,1,3,2,0:T(2,128)(2,1)}), bf16[8,2,7,7,1024]{4,1,3,2,0:T(2,128)(2,1)}, u32[]{:S(2)}, u32[]{:S(2)}) async-start(bf16[8,2,7,7,1024]{4,1,3,2,0:T(2,128)(2,1)} %copy.47), calls=%async_computation.2 | async-start | bytes 3211264 | tf_op jit(solution)/shard_map/all_to_all | solution.py:157
  26.3 0.0 copy-done.6
  26.4 1.9 convolution_convert_fusion.1
  28.2 4.5 reshape.514
  32.8 3.7 copy.42
  36.5 10.8 %all-to-all-done.2 = bf16[8,2,7,7,1024]{4,1,3,2,0:T(2,128)(2,1)} async-done(((bf16[8,2,7,7,1024]{4,1,3,2,0:T(2,128)(2,1)}), bf16[8,2,7,7,1024]{4,1,3,2,0:T(2,128)(2,1)}, u32[]{:S(2)}, u32[]{:S(2)}) %all-to-all-start.2) | async-done | bytes 1605664 | tf_op jit(solution)/shard_map/all_to_all | solution.py:157
  47.3 4.3 all-to-all-start
  51.6 0.2 all-reduce.4.cloned.1.call-start
  51.9 0.0 copy-done.7
  51.9 0.1 bitcast_multiply_fusion
  52.0 0.1 fusion.72
  52.1 4.3 copy.48
  56.4 4.7 reshape.518
  61.1 3.2 copy.52
  64.3 3.7 reshape_reshape.3
  68.0 4.6 all-to-all-done
  72.5 2.0 copy_convert_fusion
  74.5 4.5 copy.44
  79.0 5.3 %reshape.522 = f32[16,7,7,1024]{3,0,2,1:T(8,128)} reshape(f32[8,2,7,7,1024]{4,1,0,3,2:T(2,128)} %copy.44) | data formatting | bytes 6422528 | tf_op jit(solution)/shard_map/convert_element_type | solution.py:65
  84.2 26.1 %multiply_reduce_fusion.26 = (f32[16,7,7]{0,2,1:T(8,128)S(1)}, f32[16,7,7,1024]{3,0,2,1:T(8,128)S(1)}) fusion(f32[1024]{0:T(1024)S(1)} %bitcast.127, f32[1024]{0:T(1024)S(1)} %bitcast.129, f32[1024]{0:T(1024)S(1)} %bitcast.131, f32[1024]{0:T(1024)S(1)} %bitcast.133, f32[1024]{0:T(1024)S(1)} %bitcast.135, f32[1024]{0:T(1024)S(1)} %bitcast.137, ...), kind=kLoop, calls=%fused_computation.129 | loop fusion | flops 40942832 | bytes 6528064 | tf_op jit(solution)/shard_map/reduce_sum | solution.py:67
  110.4 0.0 copy-start.3
  110.4 0.0 copy-done
  110.4 0.0 copy-done.4
  110.4 0.0 copy-start.1
  110.4 4.0 multiply_convert_fusion
  114.5 0.0 copy-done.3
  114.5 0.0 copy-done.1
  114.5 9.8 %multiply_reduce_fusion = (f32[1024]{0:T(1024)S(1)}, f32[1024]{0:T(1024)S(1)}, f32[1024]{0:T(1024)S(1)}, f32[1024]{0:T(1024)S(1)}, f32[1024]{0:T(1024)S(1)}, /*i...) fusion(f32[16,7,7,1024]{3,0,2,1:T(8,128)S(1)} %copy-done.1, ...), kind=kLoop, calls=%fused_computation.98 | loop fusion | flops 32094208 | bytes 12925056 | tf_op jit(solution)/shard_map/reduce_sum | solution.py:54
  124.3 0.0 copy-start.2
  124.3 2.3 multiply_reduce_fusion.18
  126.6 0.0 copy-done.2
  126.9 0.8 multiply_bitcast_fusion
  127.7 0.0 all-reduce.4.cloned.1.call-update
  127.7 0.0 reduce-scatter.2.cloned.1.call-start
  127.8 3.6 copy.51
  131.3 3.7 reshape.521
  135.0 6.2 %convolution_bitcast_fusion = f32[1,1024,1024]{2,1,0:T(8,128)} fusion(bf16[784,1024]{1,0:T(8,128)(2,1)} %reshape.521, bf16[784,1024]{1,0:T(8,128)(2,1)} %reshape_reshape.3), kind=kOutput, calls=%fused_computation.131 | convolution fusion | flops 1644167168 | bytes 7405568 | tf_op jit(solution)/shard_map/dot_general | solution.py:96
  141.2 0.0 reduce-scatter.2.cloned.1.call-update
  141.2 6.0 %add_convert_fusion = bf16[16,7,7,1024]{3,0,2,1:T(8,128)(2,1)} fusion(f32[16,7,7,1024]{3,0,2,1:T(8,128)} %reshape.522, bf16[1,1,1024,1024]{3,2,1,0:T(8,128)(2,1)S(1)} %copy-done, f32[16,7,7,1024]{3,0,2,1:T(8,128)} %copy-done.3, f32[16,7,7]{0,2,1:T(8,128)S(1)} %add_rsqrt_fusion), kind=kOutput, calls=%fused_computation.126 | convolution fusion | flops 1650589696 | bytes 10128448 | tf_op jit(solution)/shard_map/dot_general | solution.py:69
  147.2 4.6 reshape.515
  151.8 3.7 copy.45
  155.4 4.5 all-to-all-start.1
  160.0 28.1 %fusion.47 = bf16[16,7,7,1024]{3,0,2,1:T(8,128)(2,1)} fusion(f32[16,7,7,1024]{3,0,2,1:T(8,128)} %copy-done.2, bf16[16,7,7,1024]{3,0,2,1:T(8,128)(2,1)} %reshape.518, f32[1024]{0:T(1024)S(1)} %bitcast.128, f32[1024]{0:T(1024)S(1)} %bitcast.130, f32[1024]{0:T(1024)S(1)} %bitcast.132, f32[1024]{0:T(1024)S(1)} %bitcast.134, f32[1024]{0:T(1024)S(1)} %bitcast.136, ...), kind=kLoop, calls=%fused_computation.95 | loop fusion | flops 41746432 | bytes 6524928 | tf_op jit(solution)/shard_map/convert_element_type | solution.py:89
  188.1 4.5 reshape.519
  192.7 3.7 copy.49
  196.4 0.0 all-to-all-done.1
  196.4 5.1 %all-to-all-start.3 = ((bf16[8,2,7,7,1024]{4,1,3,2,0:T(2,128)(2,1)}), bf16[8,2,7,7,1024]{4,1,3,2,0:T(2,128)(2,1)}, u32[]{:S(2)}, u32[]{:S(2)}) async-start(bf16[8,2,7,7,1024]{4,1,3,2,0:T(2,128)(2,1)} %copy.49), calls=%async_computation.3 | async-start | bytes 3211264 | tf_op jit(solution)/shard_map/all_to_all | solution.py:165
  201.5 4.3 copy.46
  205.8 4.7 reshape.516
  210.5 11.9 %all-to-all-done.3 = bf16[8,2,7,7,1024]{4,1,3,2,0:T(2,128)(2,1)} async-done(((bf16[8,2,7,7,1024]{4,1,3,2,0:T(2,128)(2,1)}), bf16[8,2,7,7,1024]{4,1,3,2,0:T(2,128)(2,1)}, u32[]{:S(2)}, u32[]{:S(2)}) %all-to-all-start.3) | async-done | bytes 1605664 | tf_op jit(solution)/shard_map/all_to_all | solution.py:165
  222.5 4.4 copy.50
  226.8 4.7 reshape.520
  231.5 2.8 convolution_convert_fusion.3
  234.4 0.0 copy-done.5
  234.4 1.3 convolution_convert_fusion.2
  235.7 149.1 %all-reduce.4.cloned.1.call-done = f32[1,1,25,1024]{3,1,2,0:T(1,128)} async-done(((f32[1,1,25,1024]{3,1,2,0:T(1,128)}), f32[1,1,25,1024]{3,1,2,0:T(1,128)}) %all-reduce.4.cloned.1.call-update) | async-done | bytes 102416 | tf_op jit(solution)/shard_map/psum | solution.py:179
  384.7 100.6 %reduce-scatter.2.cloned.1.call-done = f32[1,32,1024]{2,1,0:T(8,128)} async-done(((f32[1,1024,1024]{2,1,0:T(8,128)}), f32[1,32,1024]{2,1,0:T(8,128)}) %reduce-scatter.2.cloned.1.call-update) | async-done | bytes 131088 | tf_op jit(solution)/shard_map/reduce_scatter | solution.py:178
  485.3 1.5 copy.83
  (33 shorter events, 0.3 us)
Async XLA Ops:
  7.2 103.2 %copy-start = (bf16[1,1,1024,1024]{3,2,1,0:T(8,128)(2,1)S(1)}, bf16[1,1,1024,1024]{3,2,1,0:T(8,128)(2,1)}, u32[]{:S(2)}) copy-start(bf16[1,1,1024,1024]{3,2,1,0:T(8,128)(2,1)} %param.7) | copy-start | bytes 6291460
  16.4 10.0 %copy-start.6 = (bf16[8,7,7,1024]{3,0,2,1:T(8,128)(2,1)S(1)}, bf16[8,7,7,1024]{3,0,2,1:T(8,128)(2,1)}, u32[]{:S(2)}) copy-start(bf16[8,7,7,1024]{3,0,2,1:T(8,128)(2,1)} %param.5) | copy-start | bytes 2408452
  20.1 27.2 %all-to-all-start.2 = ((bf16[8,2,7,7,1024]{4,1,3,2,0:T(2,128)(2,1)}), bf16[8,2,7,7,1024]{4,1,3,2,0:T(2,128)(2,1)}, u32[]{:S(2)}, u32[]{:S(2)}) async-start(bf16[8,2,7,7,1024]{4,1,3,2,0:T(2,128)(2,1)} %copy.47), calls=%async_computation.2 | async-start | bytes 3211264 | tf_op jit(solution)/shard_map/all_to_all | solution.py:157
  32.8 19.2 %copy-start.7 = (f32[1,1,25,1024]{3,1,2,0:T(1,128)S(1)}, f32[1,1,25,1024]{3,1,2,0:T(1,128)}, u32[]{:S(2)}) copy-start(f32[1,1,25,1024]{3,1,2,0:T(1,128)} %param.8) | copy-start | bytes 307204
  47.3 25.2 %all-to-all-start = ((bf16[8,2,7,7,1024]{4,1,3,2,0:T(2,128)(2,1)}), bf16[8,2,7,7,1024]{4,1,3,2,0:T(2,128)(2,1)}, u32[]{:S(2)}, u32[]{:S(2)}) async-start(bf16[8,2,7,7,1024]{4,1,3,2,0:T(2,128)(2,1)} %copy.42), calls=%async_computation | async-start | bytes 3211264 | tf_op jit(solution)/shard_map/all_to_all | solution.py:137
  51.6 333.1 %all-reduce.4.cloned.1.call-start = ((), (), s32[]{:S(2)}) async-start(), calls=%async_computation.6 | async-start | bytes 204800 | tf_op jit(solution)/shard_map/psum | solution.py:179
  84.2 26.2 %copy-start.4 = (bf16[16,7,7,1024]{3,0,2,1:T(8,128)(2,1)S(1)}, bf16[16,7,7,1024]{3,0,2,1:T(8,128)(2,1)}, u32[]{:S(2)}) copy-start(bf16[16,7,7,1024]{3,0,2,1:T(8,128)(2,1)} %reshape.518) | copy-start | bytes 4816900
  110.4 4.1 copy-start.3
  110.4 4.1 copy-start.1
  124.3 2.3 copy-start.2
  127.7 357.6 %reduce-scatter.2.cloned.1.call-start = ((), (), s32[]{:S(2)}) async-start(), calls=%async_computation.5 | async-start | bytes 4325376 | tf_op jit(solution)/shard_map/reduce_scatter | solution.py:178
  155.4 40.9 %all-to-all-start.1 = ((bf16[8,2,7,7,1024]{4,1,3,2,0:T(2,128)(2,1)}), bf16[8,2,7,7,1024]{4,1,3,2,0:T(2,128)(2,1)}, u32[]{:S(2)}, u32[]{:S(2)}) async-start(bf16[8,2,7,7,1024]{4,1,3,2,0:T(2,128)(2,1)} %copy.45), calls=%async_computation.1 | async-start | bytes 3211264 | tf_op jit(solution)/shard_map/all_to_all | solution.py:141
  196.4 26.1 %all-to-all-start.3 = ((bf16[8,2,7,7,1024]{4,1,3,2,0:T(2,128)(2,1)}), bf16[8,2,7,7,1024]{4,1,3,2,0:T(2,128)(2,1)}, u32[]{:S(2)}, u32[]{:S(2)}) async-start(bf16[8,2,7,7,1024]{4,1,3,2,0:T(2,128)(2,1)} %copy.49), calls=%async_computation.3 | async-start | bytes 3211264 | tf_op jit(solution)/shard_map/all_to_all | solution.py:165
  231.5 2.9 copy-start.5
Sparse Core Ops, SparseCore 0:
  127.8 256.8 all-reduce.3
  389.7 95.5 reduce-scatter.1
where the time goes:
time: 501 us; the launch traced here: 494 us
  waiting for transfers between devices  277 us (55%)
  local copies, waits for them, and re-layouts  85.9 us (17%)
  other arithmetic  70.9 us (14%)
  matrix products  25.2 us (5%)
  starting transfers between devices  20.4 us (4%)
  between operations  14.8 us (3%)
    psum x1, waiting for transfers between devices, body(): depth_grad = lax.psum(jnp.stack(depth_parts), 'rep')  149 us
    reduce_scatter x1, waiting for transfers between devices, body(): lax.psum_scatter(jnp.stack(point_parts), 'rep', scatter_dimension=1, tile...  101 us
    convert_element_type x1, other arithmetic, block_backward(): (grad_maps.astype(jnp.float32) + depthwise_back(grad_mixed, kernel)).asty...  28.1 us
    reduce_sum x1, other arithmetic, block_forward(): jnp.mean(mixed_taps * mixed_taps, axis=-1, keepdims=True) + EPS  26.1 us
    reshape x4, local copies, waits for them, and re-layouts, body(): outgoing.reshape(sections, capacity, map_side, map_side, channels)  16.6 us
    all_to_all x2, waiting for transfers between devices, body(): lax.all_to_all(outgoing, 'segment', split_axis=0, concat_axis=0, tiled=True)  15.4 us
    reduce_sum x2, other arithmetic, kernel_grad(): jnp.sum(grad_maps * shift_window(padded, offset // 5 - 2, offset % 5 - 2,...  12.1 us
    all_to_all x1, waiting for transfers between devices, body(): lax.all_to_all(grad_in.reshape(sections, capacity, map_side, map_side, ch...  11.9 us
  transfers between devices with their start and end apart: 6, of which 5 were waited for; matrix products, arithmetic and copies ran while one was open for 23% of the time, Pallas kernels for 0%

commit v1 on v0

v1 whole, which is shorter than its diff:
```python
import functools

import jax
import jax.numpy as jnp
from jax import lax
from jax.experimental import pallas as pl
from jax.experimental.pallas import tpu as pltpu
from jax.sharding import PartitionSpec as P

MESH = pl.DeviceIdType.MESH
EPS = 1e-05
F32 = jnp.float32
BF16 = jnp.bfloat16

C = 1024
SIDE = 7
POS = SIDE * SIDE
MAIN = 48
ROWS = 400
LANES = 128
SEG = 8
PARTNERS = ((1, 0), (0, 1), (0, 3), (1, 1), (1, 3), (0, 2), (1, 2))

XM0, XM1, XL, GM0, GM1, GL, OM0, OM1, OL, IM0, IM1, IL = range(12)


def iota2(rows, cols):
    return (
        lax.broadcasted_iota(jnp.int32, (rows, cols), 0),
        lax.broadcasted_iota(jnp.int32, (rows, cols), 1),
    )


def onehot(cond):
    return jnp.where(cond, 1.0, 0.0)


def mm(a, b):
    return jnp.dot(a, b, preferred_element_type=F32)


def kernel(
    slot_ref,
    x_ref,
    g_ref,
    w_ref,
    k_ref,
    out_ref,
    gin_ref,
    pgrad_ref,
    dgrad_ref,
    sx, rx, sxl, rxl,
    sg, rg, sgl, rgl,
    so, ro, sol, rol,
    si, ri, sil, ril,
    x32, h32, gh32, g32, ab, gb, q128, kb,
    fold_o, fold_i,
    pg, prx, psb, prb, psc, prc,
    dka, dkb, dky, dkz,
    send_sem, recv_sem, local_sem, rsend, rrecv,
):
    me = lax.axis_index("segment")
    rep = lax.axis_index("rep")
    z_lo = me // 4
    xx = me % 4
    my_y = rep // 8
    my_z = (rep // 2) % 4
    core = rep % 2

    def seg_at(dz, dx):
        return ((z_lo + dz) % 2) * 4 + (xx + dx) % 4

    def rep_at(dy, dz, dc):
        return ((my_y + dy) % 4) * 8 + ((my_z + dz) % 4) * 2 + (core + dc) % 2

    rep_partners = ((0, 0, 1), (1, 0, 0), (2, 0, 0), (3, 0, 0), (0, 1, 0), (0, 2, 0), (0, 3, 0))

    barrier = pltpu.get_barrier_semaphore()
    for dz, dx in PARTNERS:
        pl.semaphore_signal(barrier, inc=1, device_id=(seg_at(dz, dx), rep), device_id_type=MESH)
    for dy, dz, dc in rep_partners:
        pl.semaphore_signal(
            barrier, inc=1, device_id=(me, rep_at(dy, dz, dc)), device_id_type=MESH
        )

    def seg_copy(kind, src, dst, there, slot):
        return pltpu.make_async_remote_copy(
            src_ref=src.at[there],
            dst_ref=dst.at[slot],
            send_sem=send_sem.at[kind, there],
            recv_sem=recv_sem.at[kind, slot],
            device_id=(there, rep),
            device_id_type=MESH,
        )

    def seg_send(kind, src, dst):
        for dz, dx in PARTNERS:
            seg_copy(kind, src, dst, seg_at(dz, dx), me).start()
        pltpu.make_async_copy(src.at[me], dst.at[me], local_sem.at[kind]).start()

    def seg_wait(kind, src, dst):
        pltpu.make_async_copy(src.at[me], dst.at[me], local_sem.at[kind]).wait()
        for dz, dx in PARTNERS:
            there = seg_at(dz, dx)
            seg_copy(kind, src, dst, there, there).wait_recv()

    def seg_sent(kind, src, dst):
        for dz, dx in PARTNERS:
            seg_copy(kind, src, dst, seg_at(dz, dx), me).wait_send()

    m, n = iota2(256, 128)
    slots = jnp.broadcast_to(slot_ref[...], (256, 128))
    wanted = 2 * ((m >> 4) & 7) + (m >> 7)
    route32 = onehot(((m & 15) == (n >> 3)) & (slots == wanted))
    route = route32.astype(BF16)
    route_back = route32.T.astype(BF16)
    m, n = iota2(128, 128)
    slots = jnp.broadcast_to(slot_ref[...], (128, 128))
    route_last32 = onehot(((m & 7) == (n >> 3)) & (slots == (m >> 3)))
    route_last = route_last32.astype(BF16)
    route_last_back = route_last32.T.astype(BF16)
    to_rows = onehot(((m >> 3) == (n & 15)) & ((m & 7) == (n >> 4))).astype(BF16)
    from_rows = onehot(((m & 15) == (n >> 3)) & ((m >> 4) == (n & 7))).astype(BF16)
    unfold = onehot(
        ((m >> 4) == (n & 7)) & (((m >> 3) & 1) == ((n >> 3) & 1)) & ((m & 7) == (n >> 4))
    ).astype(BF16)
    refold = onehot(
        ((n >> 4) == (m & 7)) & (((n >> 3) & 1) == ((m >> 3) & 1)) & ((n & 7) == (m >> 4))
    ).astype(BF16)

    def dispatch(source, main, last):
        for q in range(3):
            for part in range(4):
                lanes = slice(part * 256, part * 256 + 256)
                moved = mm(route, source[q * 128 : q * 128 + 128, lanes]).astype(BF16)
                for j in range(2):
                    main[j, :, q * 16 : q * 16 + 16, lanes] = moved[
                        j * 128 : j * 128 + 128
                    ].reshape(8, 16, 256)
        tail = source[384:392, :].astype(F32)
        folded = jnp.concatenate(
            [tail[:, b * LANES : b * LANES + LANES] for b in range(8)]
            + [jnp.zeros((64, LANES), F32)],
            axis=0,
        ).astype(BF16)
        last[...] = mm(route_last, folded).astype(BF16).reshape(8, 16, LANES)

    dispatch(x_ref, sx, sxl)
    pl.semaphore_wait(barrier, 14)
    seg_send(XM0, sx.at[0], rx.at[0])
    seg_send(XL, sxl, rxl)
    dispatch(g_ref, sg, sgl)
    seg_send(GM0, sg.at[0], rg.at[0])
    seg_send(GL, sgl, rgl)
    seg_send(XM1, sx.at[1], rx.at[1])
    seg_send(GM1, sg.at[1], rg.at[1])

    kb[...] = jnp.broadcast_to(k_ref[...][:, None, :], (25, 8, C))
    dka[...] = jnp.zeros((25, 8, C), F32)
    for j in range(2):
        x32[j, 392:400, :] = jnp.zeros((8, C), F32)
        h32[j, 392:400, :] = jnp.zeros((8, C), F32)

    def receive_main(j, got, wide, narrow):
        for q in range(3):
            for part in range(4):
                lanes = slice(part * 256, part * 256 + 256)
                rows = mm(to_rows, got[j, :, q * 16 : q * 16 + 16, lanes].reshape(128, 256))
                wide[j, q * 128 : q * 128 + 128, lanes] = rows
                if narrow is not None:
                    narrow[j, q * 128 : q * 128 + 128, lanes] = rows.astype(BF16)

    def receive_last(got, wide, narrow):
        rows = mm(unfold, got[...].reshape(128, LANES))
        for j in range(2):
            row = jnp.concatenate(
                [rows[b * 16 + j * 8 : b * 16 + j * 8 + 8] for b in range(8)], axis=1
            )
            wide[j, 384:392, :] = row
            if narrow is not None:
                narrow[j, 384:400, :] = jnp.concatenate([row, jnp.zeros((8, C), F32)], 0).astype(BF16)

    def rows_at(ref, j, r, lanes):
        return [ref[j, (r * 7 + c) * 8 : (r * 7 + c) * 8 + 8, lanes] for c in range(7)]

    def convolve(j, source, sign, emit):
        def body(block, carry):
            lanes = pl.ds(pl.multiple_of(block * LANES, LANES), LANES)
            for r in range(7):
                acc = [None] * 7
                for dr in range(-2, 3):
                    at = r + sign * dr
                    if at < 0 or at > 6:
                        continue
                    row = rows_at(source, j, at, lanes)
                    for dc in range(-2, 3):
                        tap = kb[(dr + 2) * 5 + dc + 2, :, lanes]
                        for c in range(7):
                            ac = c + sign * dc
                            if ac < 0 or ac > 6:
                                continue
                            term = tap * row[ac]
                            acc[c] = term if acc[c] is None else acc[c] + term
                for c in range(7):
                    emit(j, (r * 7 + c) * 8, lanes, acc[c])
            return carry

        lax.fori_loop(0, 8, body, 0)

    def emit_h(j, row, lanes, value):
        h32[j, row : row + 8, lanes] = value

    def emit_gin(j, row, lanes, value):
        g32[j, row : row + 8, lanes] = g32[j, row : row + 8, lanes] + value

    def tap_grad(j):
        def body(block, carry):
            lanes = pl.ds(pl.multiple_of(block * LANES, LANES), LANES)
            for dr in range(-2, 3):
                acc = [None] * 5
                for r in range(7):
                    at = r + dr
                    if at < 0 or at > 6:
                        continue
                    grad = rows_at(gh32, j, r, lanes)
                    row = rows_at(x32, j, at, lanes)
                    for dc in range(-2, 3):
                        for c in range(7):
                            ac = c + dc
                            if ac < 0 or ac > 6:
                                continue
                            term = grad[c] * row[ac]
                            acc[dc + 2] = term if acc[dc + 2] is None else acc[dc + 2] + term
                for t in range(5):
                    at = (dr + 2) * 5 + t
                    dka[at, :, lanes] = dka[at, :, lanes] + acc[t]
            return carry

        lax.fori_loop(0, 8, body, 0)

    def activate(j):
        def body(step, carry):
            rows = pl.ds(pl.multiple_of(step * 80, 80), 80)
            h = h32[j, rows, :]
            q = lax.rsqrt(jnp.sum(h * h, axis=1, keepdims=True) * (1.0 / C) + EPS)
            z = h * q
            h32[j, rows, :] = z
            q128[j, rows, :] = jnp.broadcast_to(q, (80, LANES))
            ab[j, rows, :] = (z * jax.nn.sigmoid(z)).astype(BF16)
            return carry

        lax.fori_loop(0, 5, body, 0)

    def send_rows(j, value, n, main, fold):
        lanes = pl.ds(pl.multiple_of(n * 256, 256), 256)
        for q in range(3):
            moved = mm(from_rows, value[q * 128 : q * 128 + 128]).astype(BF16)
            main[j, :, q * 16 : q * 16 + 16, lanes] = moved.reshape(8, 16, 256)
        tail = value[384:400].astype(F32)
        for b in range(2):
            fold[pl.ds(pl.multiple_of((2 * n + b) * 16 + j * 8, 8), 8), :] = tail[
                :8, b * LANES : b * LANES + LANES
            ]

    def send_last(fold, last):
        last[...] = mm(refold, fold[...].astype(BF16)).astype(BF16).reshape(8, 16, LANES)

    def project(j):
        def body(n, carry):
            lanes = pl.ds(pl.multiple_of(n * 256, 256), 256)
            value = (x32[j, :, lanes] + mm(ab[j], w_ref[:, lanes])).astype(BF16)
            send_rows(j, value, n, so, fold_o)
            return carry

        lax.fori_loop(0, 4, body, 0)

    def back_project(j):
        def body(n, carry):
            lanes = pl.ds(pl.multiple_of(n * 256, 256), 256)
            gh32[j, :, lanes] = lax.dot_general(
                gb[j], w_ref[lanes, :], (((1,), (1,)), ((), ())), preferred_element_type=F32
            )
            return carry

        lax.fori_loop(0, 4, body, 0)

    def back_activate(j):
        def body(step, carry):
            rows = pl.ds(pl.multiple_of(step * 80, 80), 80)
            z = h32[j, rows, :]
            s = jax.nn.sigmoid(z)
            gz = gh32[j, rows, :] * s * (1.0 + z * (1.0 - s))
            mean = jnp.sum(gz * z, axis=1, keepdims=True) * (1.0 / C)
            q = jnp.concatenate([q128[j, rows, :]] * 8, axis=1)
            gh32[j, rows, :] = q * (gz - z * mean)
            return carry

        lax.fori_loop(0, 5, body, 0)

    def send_gin(j):
        def body(n, carry):
            lanes = pl.ds(pl.multiple_of(n * 256, 256), 256)
            send_rows(j, g32[j, :, lanes].astype(BF16), n, si, fold_i)
            return carry

        lax.fori_loop(0, 4, body, 0)

    def forward(j):
        seg_wait((XM0, XM1)[j], sx.at[j], rx.at[j])
        receive_main(j, rx, x32, None)
        if j == 0:
            seg_wait(XL, sxl, rxl)
            receive_last(rxl, x32, None)
        convolve(j, x32, 1, emit_h)
        activate(j)
        project(j)
        seg_send((OM0, OM1)[j], so.at[j], ro.at[j])
        if j == 1:
            send_last(fold_o, sol)
            seg_send(OL, sol, rol)

    def receive_g(j):
        seg_wait((GM0, GM1)[j], sg.at[j], rg.at[j])
        receive_main(j, rg, g32, gb)
        if j == 0:
            seg_wait(GL, sgl, rgl)
            receive_last(rgl, g32, gb)
            for i in range(2):
                g32[i, 392:400, :] = jnp.zeros((8, C), F32)

    def backward(j):
        back_project(j)
        back_activate(j)
        convolve(j, gh32, -1, emit_gin)
        send_gin(j)
        seg_send((IM0, IM1)[j], si.at[j], ri.at[j])

    def home(main, last, target):
        for q in range(3):
            for part in range(4):
                lanes = slice(part * 256, part * 256 + 256)
                got = jnp.concatenate(
                    [main[j, :, q * 16 : q * 16 + 16, lanes].reshape(128, 256) for j in range(2)],
                    axis=0,
                )
                target[q * 128 : q * 128 + 128, lanes] = mm(route_back, got).astype(BF16)
        rows = mm(route_last_back, last[...].reshape(128, LANES))
        target[384:392, :] = jnp.concatenate(
            [rows[b * 8 : b * 8 + 8] for b in range(8)], axis=1
        ).astype(BF16)

    def rep_copy(kind, src, dst, dy, dz, dc):
        return pltpu.make_async_remote_copy(
            src_ref=src,
            dst_ref=dst,
            send_sem=rsend.at[kind],
            recv_sem=rrecv.at[kind],
            device_id=(me, rep_at(dy, dz, dc)),
            device_id_type=MESH,
        )

    sibling = (core + 1) % 2

    def pair_copy(y):
        return rep_copy(y, pg.at[y, :, sibling], prx.at[y], 0, 0, 1)

    def point_terms():
        for y in range(4):
            cols = slice(y * 256, y * 256 + 256)
            for part in range(4):
                lanes = slice(part * 256, part * 256 + 256)
                total = None
                for j in range(2):
                    term = lax.dot_general(
                        ab[j, :, cols],
                        gb[j, :, lanes],
                        (((0,), (0,)), ((), ())),
                        preferred_element_type=F32,
                    )
                    total = term if total is None else total + term
                pg[y, :, :, :, lanes] = total.reshape(4, 2, 32, 256)
            pair_copy(y).start()

    def y_copy(dy):
        return rep_copy(3 + dy, psb.at[dy - 1], prb.at[dy - 1], dy, 0, 0)

    def z_copy(dz):
        return rep_copy(6 + dz, psc.at[dz - 1], prc.at[dz - 1], 0, dz, 0)

    def point_over_y():
        for dy in (1, 2, 3, 0):
            y = (my_y + dy) % 4
            pair_copy(y).wait_recv()
            total = pg[y, :, core] + prx[y]
            if dy:
                psb[dy - 1] = total.astype(BF16)
                y_copy(dy).start()
            else:
                prx[y] = total

    def point_over_z():
        total = prx[my_y]
        for dy in (1, 2, 3):
            y_copy(dy).wait_recv()
        for slot in range(3):
            total = total + prb[slot].astype(F32)
        prx[my_y] = total
        for dz in (1, 2, 3):
            psc[dz - 1] = prx[my_y, (my_z + dz) % 4].astype(BF16)
            z_copy(dz).start()

    def point_end():
        for dz in (1, 2, 3):
            z_copy(dz).wait_recv()
        total = prx[my_y, my_z]
        for slot in range(3):
            total = total + prc[slot].astype(F32)
        pgrad_ref[...] = total

    def tap_pair():
        return rep_copy(10, dkb.at[0], dkb.at[1], 0, 0, 1)

    def tap_y(dy, slot):
        return rep_copy(10 + dy, dky.at[my_y], dky.at[slot], dy, 0, 0)

    def tap_z(dz, slot):
        return rep_copy(13 + dz, dkz.at[my_z], dkz.at[slot], 0, dz, 0)

    forward(0)
    receive_g(0)
    backward(0)
    forward(1)
    receive_g(1)
    point_terms()
    back_project(1)
    back_activate(1)
    point_over_y()
    tap_grad(0)
    tap_grad(1)
    dkb[0] = jnp.concatenate([jnp.sum(dka[...], axis=1), jnp.zeros((7, C), F32)], axis=0)
    tap_pair().start()
    convolve(1, gh32, -1, emit_gin)
    send_gin(1)
    seg_send(IM1, si.at[1], ri.at[1])
    send_last(fold_i, sil)
    seg_send(IL, sil, ril)
    point_over_z()
    tap_pair().wait_recv()
    dky[my_y] = dkb[0] + dkb[1]
    for dy in (1, 2, 3):
        tap_y(dy, my_y).start()

    seg_wait(OM0, so.at[0], ro.at[0])
    seg_wait(OM1, so.at[1], ro.at[1])
    seg_wait(OL, sol, rol)
    home(ro, rol, out_ref)
    for dy in (1, 2, 3):
        tap_y(dy, (my_y + 4 - dy) % 4).wait_recv()
    dkz[my_z] = (dky[0] + dky[1]) + (dky[2] + dky[3])
    for dz in (1, 2, 3):
        tap_z(dz, my_z).start()
    point_end()
    seg_wait(IM0, si.at[0], ri.at[0])
    seg_wait(IM1, si.at[1], ri.at[1])
    seg_wait(IL, sil, ril)
    home(ri, ril, gin_ref)
    for dz in (1, 2, 3):
        tap_z(dz, (my_z + 4 - dz) % 4).wait_recv()
    dgrad_ref[...] = ((dkz[0] + dkz[1]) + (dkz[2] + dkz[3]))[:25]

    for j in range(2):
        seg_sent((XM0, XM1)[j], sx.at[j], rx.at[j])
        seg_sent((GM0, GM1)[j], sg.at[j], rg.at[j])
        seg_sent((OM0, OM1)[j], so.at[j], ro.at[j])
        seg_sent((IM0, IM1)[j], si.at[j], ri.at[j])
    seg_sent(XL, sxl, rxl)
    seg_sent(GL, sgl, rgl)
    seg_sent(OL, sol, rol)
    seg_sent(IL, sil, ril)
    for y in range(4):
        pair_copy(y).wait_send()
    tap_pair().wait_send()
    for d in (1, 2, 3):
        y_copy(d).wait_send()
        z_copy(d).wait_send()
        tap_y(d, my_y).wait_send()
        tap_z(d, my_z).wait_send()


def tap_mask(op_kind):
    tap_index = jnp.arange(25, dtype=jnp.int32)
    row_shift = tap_index // 5 - 2
    col_shift = tap_index % 5 - 2
    narrow = (jnp.abs(row_shift) <= 1) & (jnp.abs(col_shift) <= 1)
    spaced = (row_shift % 2 == 0) & (col_shift % 2 == 0)
    tap_keep = jnp.where(op_kind == 0, narrow, jnp.where(op_kind == 1, True, spaced))
    return tap_keep.astype(jnp.float32)


def body(feature_maps, path_lists, point_weight, depth_kernel, cotangent):
    section = lax.axis_index("segment")
    path = path_lists[0, :, 0]
    index = jnp.arange(8, dtype=jnp.int32)
    same = (path[None, :] == path[:, None]) & (index[None, :] < index[:, None])
    slot = path * 2 + jnp.sum(same.astype(jnp.int32), axis=1)
    slots = jnp.tile(slot, 16)[None, :]
    keep = tap_mask(section % 3)[:, None]
    x = feature_maps.transpose(1, 2, 0, 3).reshape(POS * 8, C)
    g = cotangent.transpose(1, 2, 0, 3).reshape(POS * 8, C)
    vmem = pl.BlockSpec(memory_space=pltpu.VMEM)
    main = pltpu.VMEM((2, SEG, MAIN, C), BF16)
    last = pltpu.VMEM((SEG, 16, LANES), BF16)
    wide = pltpu.VMEM((2, ROWS, C), F32)
    narrow = pltpu.VMEM((2, ROWS, C), BF16)
    out, gin, pgrad, dgrad = pl.pallas_call(
        kernel,
        out_shape=(
            jax.ShapeDtypeStruct((POS * 8, C), BF16),
            jax.ShapeDtypeStruct((POS * 8, C), BF16),
            jax.ShapeDtypeStruct((32, C), F32),
            jax.ShapeDtypeStruct((25, C), F32),
        ),
        in_specs=[vmem] * 5,
        out_specs=[vmem] * 4,
        scratch_shapes=[
            *[main, main, last, last] * 4,
            wide, wide, wide, wide, narrow, narrow,
            pltpu.VMEM((2, ROWS, LANES), F32),
            pltpu.VMEM((25, 8, C), F32),
            pltpu.VMEM((128, LANES), F32),
            pltpu.VMEM((128, LANES), F32),
            pltpu.VMEM((4, 4, 2, 32, C), F32),
            pltpu.VMEM((4, 4, 32, C), F32),
            pltpu.VMEM((3, 4, 32, C), BF16),
            pltpu.VMEM((3, 4, 32, C), BF16),
            pltpu.VMEM((3, 32, C), BF16),
            pltpu.VMEM((3, 32, C), BF16),
            pltpu.VMEM((25, 8, C), F32),
            pltpu.VMEM((2, 32, C), F32),
            pltpu.VMEM((4, 32, C), F32),
            pltpu.VMEM((4, 32, C), F32),
            pltpu.SemaphoreType.DMA((12, SEG)),
            pltpu.SemaphoreType.DMA((12, SEG)),
            pltpu.SemaphoreType.DMA((12,)),
            pltpu.SemaphoreType.DMA((17,)),
            pltpu.SemaphoreType.DMA((17,)),
        ],
        compiler_params=pltpu.CompilerParams(
            collective_id=0, has_side_effects=True, vmem_limit_bytes=60 * 1024 * 1024
        ),
        name="supernet_window",
    )(slots, x, g, point_weight[0, 0], depth_kernel[0, 0] * keep)
    final = out.reshape(SIDE, SIDE, 8, C).transpose(2, 0, 1, 3)
    grad = gin.reshape(SIDE, SIDE, 8, C).transpose(2, 0, 1, 3)
    return final, grad, pgrad[None, None], (dgrad * keep)[None, None]


def solution(mesh):
    placed = (
        P(("segment", "rep"), None, None, None),
        P(None, ("segment", "rep"), None),
        P(None, "segment", None, None),
        P(None, "segment", None, None),
        P(("segment", "rep"), None, None, None),
    )
    return jax.shard_map(
        body,
        mesh=mesh,
        in_specs=placed,
        out_specs=(
            P(("segment", "rep"), None, None, None),
            P(("segment", "rep"), None, None, None),
            P(None, "segment", "rep", None),
            P(None, "segment", None, None),
        ),
        check_vma=False,
    )
```

time: 501 us -> 111 us (0.22); the launches traced: 494 us -> 110 us
  waiting for transfers between devices: 277 us -> 0 us
  Pallas kernels: 0 us -> 100 us
  local copies, waits for them, and re-layouts: 85.9 us -> 4.98 us
  other arithmetic: 70.9 us -> 4.28 us
  matrix products: 25.2 us -> 0 us
  starting transfers between devices: 20.4 us -> 0 us
  between operations: 14.8 us -> 0.69 us
    psum x1 -> x0, waiting for transfers between devices: 149 us -> none  [body(): depth_grad = lax.psum(jnp.stack(depth_parts), 'rep')]
    reduce_scatter x1 -> x0, waiting for transfers between devices: 101 us -> none  [body(): lax.psum_scatter(jnp.stack(point_parts), 'rep', scatter_dimension=1, tile...]
    pallas_call x0 -> x1, Pallas kernels: none -> 100 us  [body(): pl.pallas_call(kernel, out_shape=(jax.ShapeDtypeStruct((POS * 8, C), BF16...]
    reshape x12 -> x0, local copies, waits for them, and re-layouts: 50.8 us -> none  [the longest x4 16.6 us: body(): outgoing.reshape(sections, capacity, map_side, map_side, channels)]
    reduce_sum x4 -> x1, other arithmetic: 39.2 us -> 0.91 us  [body(): slot = path * 2 + jnp.sum(same.astype(jnp.int32), axis=1)]
    convert_element_type x2 -> x0, other arithmetic: 30.1 us -> none  [the longest x1 28.1 us: block_backward(): (grad_maps.astype(jnp.float32) + depthwise_back(grad_mixed, kernel)).asty...]
    all_to_all x4 -> x0, waiting for transfers between devices: 27.3 us -> none  [the longest x2 15.4 us: body(): lax.all_to_all(outgoing, 'segment', split_axis=0, concat_axis=0, tiled=True)]
    dot_general x7 -> x0, matrix products: 25.2 us -> none  [the longest x1 6.21 us: point_term(): lax.dot_general(active, flat_grads, (((0,), (0,)), ((), ())), preferred_e...]
  transfers between devices with their start and end apart: 6 -> 0, of which waited for: 5 -> 0; matrix products, arithmetic and copies ran while one was open for 23% -> 0% of each run, Pallas kernels for 0% -> 0%
where the time goes in v1:
time: 111 us; the launch traced here: 110 us
  Pallas kernels  100 us (90%)
  local copies, waits for them, and re-layouts  4.98 us (4%)
  other arithmetic  4.28 us (4%)
    pallas_call x1, Pallas kernels, body(): pl.pallas_call(kernel, out_shape=(jax.ShapeDtypeStruct((POS * 8, C), BF16...  100 us
    unnamed x8, local copies, waits for them, and re-layouts  4.37 us

profile of v1, /device:TPU:1, one launch (start us, length us, event | category | flops | bytes accessed | tf_op | source)
XLA Modules:
  0.0 110.4 jit_solution(10614172428700473746)
XLA Ops:
  0.7 1.6 %bitcast_multiply_fusion.k_ref = f32[25,1024]{1,0:T(8,128)} fusion(f32[1,1,25,1024]{3,1,2,0:T(1,128)} %param.8, f32[25]{0:T(128)S(1)} %select_convert_fusion), kind=kLoop, calls=%fused_computation | loop fusion | flops 25600 | bytes 204900 | tf_op jit(solution)/shard_map/mul | solution.py:552
  2.3 0.9 convert_reduce_fusion
  3.2 0.7 multiply_add_fusion
  3.9 0.6 broadcast_in_dim_tile.3.slot_ref
  4.5 100.4 %supernet_window.1 = (bf16[392,1024]{1,0:T(8,128)(2,1)}, bf16[392,1024]{1,0:T(8,128)(2,1)}, f32[32,1024]{1,0:T(8,128)}, f32[25,1024]{1,0:T(8,128)}) custom-call(s32[1,128]{1,0:T(1,128)} %broadcast_in_dim_tile.3.slot_ref, bf16[392,1024]{1,0:T(8,128)(2,1)} %bitcast.23, bf16[392,1024]{1,0:T(8,128)(2,1)} %bitcast.24, bf16[1024,1024]{1,0:T(8,128)(2,1)} %bitcast.20, ...), custom_call_target="tpu_custom_call" | custom-call | tf_op jit(solution)/shard_map/supernet_window/pallas_call | solution.py:515
  104.9 0.0 copy-start
  104.9 0.0 copy-start.1
  104.9 1.1 multiply_bitcast_fusion
  106.0 0.7 copy.11
  106.7 2.1 %copy.17 = bf16[8,7,7,1024]{3,0,2,1:T(8,128)(2,1)} copy(bf16[8,7,7,1024]{3,0,2,1:T(8,128)(2,1)} %bitcast.22) | data formatting | bytes 1605632
  108.8 0.0 copy-done
  108.8 0.9 copy.18
  109.7 0.0 copy-done.1
  109.7 0.7 copy.19
  (2 shorter events, 0.0 us)
Async XLA Ops:
  104.9 3.9 %copy-start = (bf16[392,1024]{1,0:T(8,128)(2,1)S(1)}, bf16[392,1024]{1,0:T(8,128)(2,1)}, u32[]{:S(2)}) copy-start(bf16[392,1024]{1,0:T(8,128)(2,1)} %get-tuple-element.9) | copy-start | bytes 2408452
  104.9 4.8 %copy-start.1 = (f32[32,1024]{1,0:T(8,128)S(1)}, f32[32,1024]{1,0:T(8,128)}, u32[]{:S(2)}) copy-start(f32[32,1024]{1,0:T(8,128)} %get-tuple-element.10) | copy-start | bytes 393220

commit v2 on v1

--- a/solution.py
+++ b/solution.py
@@ -40,7 +40,7 @@
 
 
 def kernel(
-    slot_ref,
+    path_ref,
     x_ref,
     g_ref,
     w_ref,
@@ -56,7 +56,7 @@
     x32, h32, gh32, g32, ab, gb, q128, kb,
     fold_o, fold_i,
     pg, prx, psb, prb, psc, prc,
-    dka, dkb, dky, dkz,
+    dka, tap_own, tap_pair_in, tap_y_in, tap_z_all, tap_all,
     send_sem, recv_sem, local_sem, rsend, rrecv,
 ):
     me = lax.axis_index("segment")
@@ -108,14 +108,28 @@
         for dz, dx in PARTNERS:
             seg_copy(kind, src, dst, seg_at(dz, dx), me).wait_send()
 
+    paths = [path_ref[0, i] for i in range(8)]
+    slot_of = []
+    for i in range(8):
+        rank = jnp.int32(0)
+        for earlier in range(i):
+            rank = rank + jnp.where(paths[earlier] == paths[i], 1, 0)
+        slot_of.append(2 * paths[i] + rank)
+
+    def slots_like(sample):
+        slots = jnp.full(sample.shape, -1, jnp.int32)
+        for i in range(8):
+            slots = jnp.where(sample == i, slot_of[i], slots)
+        return slots
+
     m, n = iota2(256, 128)
-    slots = jnp.broadcast_to(slot_ref[...], (256, 128))
+    slots = slots_like(n & 7)
     wanted = 2 * ((m >> 4) & 7) + (m >> 7)
     route32 = onehot(((m & 15) == (n >> 3)) & (slots == wanted))
     route = route32.astype(BF16)
     route_back = route32.T.astype(BF16)
     m, n = iota2(128, 128)
-    slots = jnp.broadcast_to(slot_ref[...], (128, 128))
+    slots = slots_like(n & 7)
     route_last32 = onehot(((m & 7) == (n >> 3)) & (slots == (m >> 3)))
     route_last = route_last32.astype(BF16)
     route_last_back = route_last32.T.astype(BF16)
@@ -155,7 +169,14 @@
     seg_send(XM1, sx.at[1], rx.at[1])
     seg_send(GM1, sg.at[1], rg.at[1])
 
-    kb[...] = jnp.broadcast_to(k_ref[...][:, None, :], (25, 8, C))
+    kind = me % 3
+    keep = []
+    for t in range(25):
+        row, col = t // 5 - 2, t % 5 - 2
+        narrow = 1.0 if abs(row) <= 1 and abs(col) <= 1 else 0.0
+        spaced = 1.0 if row % 2 == 0 and col % 2 == 0 else 0.0
+        keep.append(jnp.where(kind == 0, narrow, jnp.where(kind == 1, 1.0, spaced)))
+        kb[t] = jnp.broadcast_to(k_ref[t], (8, C)) * keep[t]
     dka[...] = jnp.zeros((25, 8, C), F32)
     for j in range(2):
         x32[j, 392:400, :] = jnp.zeros((8, C), F32)
@@ -364,22 +385,24 @@
     def pair_copy(y):
         return rep_copy(y, pg.at[y, :, sibling], prx.at[y], 0, 0, 1)
 
-    def point_terms():
-        for y in range(4):
-            cols = slice(y * 256, y * 256 + 256)
+    def point_terms(j):
+        for dy in (1, 2, 3, 0):
+            y = (my_y + dy) % 4
+            cols = pl.ds(pl.multiple_of(y * 256, 256), 256)
             for part in range(4):
                 lanes = slice(part * 256, part * 256 + 256)
-                total = None
-                for j in range(2):
-                    term = lax.dot_general(
-                        ab[j, :, cols],
-                        gb[j, :, lanes],
-                        (((0,), (0,)), ((), ())),
-                        preferred_element_type=F32,
-                    )
-                    total = term if total is None else total + term
-                pg[y, :, :, :, lanes] = total.reshape(4, 2, 32, 256)
-            pair_copy(y).start()
+                term = lax.dot_general(
+                    ab[j, :, cols],
+                    gb[j, :, lanes],
+                    (((0,), (0,)), ((), ())),
+                    preferred_element_type=F32,
+                ).reshape(4, 2, 32, 256)
+                if j == 0:
+                    pg[y, :, :, :, lanes] = term
+                else:
+                    pg[y, :, :, :, lanes] = pg[y, :, :, :, lanes] + term
+            if j == 1:
+                pair_copy(y).start()
 
     def y_copy(dy):
         return rep_copy(3 + dy, psb.at[dy - 1], prb.at[dy - 1], dy, 0, 0)
@@ -418,55 +441,92 @@
         pgrad_ref[...] = total
 
     def tap_pair():
-        return rep_copy(10, dkb.at[0], dkb.at[1], 0, 0, 1)
-
-    def tap_y(dy, slot):
-        return rep_copy(10 + dy, dky.at[my_y], dky.at[slot], dy, 0, 0)
+        return rep_copy(10, tap_own.at[sibling], tap_pair_in, 0, 0, 1)
+
+    def tap_y(dy):
+        return rep_copy(10 + dy, tap_own.at[core, (my_y + dy) % 4], tap_y_in.at[dy - 1], dy, 0, 0)
 
     def tap_z(dz, slot):
-        return rep_copy(13 + dz, dkz.at[my_z], dkz.at[slot], 0, dz, 0)
+        return rep_copy(13 + dz, tap_z_all.at[my_z], tap_z_all.at[slot], 0, dz, 0)
+
+    def tap_back_y(dy, slot):
+        return rep_copy(16 + dy, tap_all.at[core, my_y], tap_all.at[core, slot], dy, 0, 0)
+
+    def tap_back_pair(slot):
+        return rep_copy(20, tap_all.at[core], tap_all.at[slot], 0, 0, 1)
+
+    def taps_to_pair():
+        sums = jnp.concatenate([jnp.sum(dka[...], axis=1), jnp.zeros((7, C), F32)], axis=0)
+        for block in range(8):
+            tap_own[block // 4, block % 4] = sums[:, block * LANES : block * LANES + LANES]
+        tap_pair().start()
+
+    def taps_to_y():
+        tap_pair().wait_recv()
+        tap_own[core] = tap_own[core] + tap_pair_in[...]
+        for dy in (1, 2, 3):
+            tap_y(dy).start()
+
+    def taps_to_z():
+        total = tap_own[core, my_y]
+        for dy in (1, 2, 3):
+            tap_y(dy).wait_recv()
+            total = total + tap_y_in[dy - 1]
+        tap_z_all[my_z] = total
+        for dz in (1, 2, 3):
+            tap_z(dz, my_z).start()
+
+    def taps_back_y():
+        for dz in (1, 2, 3):
+            tap_z(dz, (my_z + 4 - dz) % 4).wait_recv()
+        tap_all[core, my_y] = (tap_z_all[0] + tap_z_all[1]) + (tap_z_all[2] + tap_z_all[3])
+        for dy in (1, 2, 3):
+            tap_back_y(dy, my_y).start()
+
+    def taps_back_pair():
+        for dy in (1, 2, 3):
+            tap_back_y(dy, (my_y + 4 - dy) % 4).wait_recv()
+        tap_back_pair(core).start()
+
+    def taps_end():
+        tap_back_pair(sibling).wait_recv()
+        sums = jnp.concatenate([tap_all[b // 4, b % 4] for b in range(8)], axis=1)
+        for t in range(25):
+            dgrad_ref[t] = sums[t : t + 1] * keep[t]
 
     forward(0)
     receive_g(0)
     backward(0)
+    tap_grad(0)
+    point_terms(0)
     forward(1)
     receive_g(1)
-    point_terms()
+    point_terms(1)
     back_project(1)
     back_activate(1)
     point_over_y()
-    tap_grad(0)
-    tap_grad(1)
-    dkb[0] = jnp.concatenate([jnp.sum(dka[...], axis=1), jnp.zeros((7, C), F32)], axis=0)
-    tap_pair().start()
     convolve(1, gh32, -1, emit_gin)
     send_gin(1)
     seg_send(IM1, si.at[1], ri.at[1])
     send_last(fold_i, sil)
     seg_send(IL, sil, ril)
+    tap_grad(1)
+    taps_to_pair()
     point_over_z()
-    tap_pair().wait_recv()
-    dky[my_y] = dkb[0] + dkb[1]
-    for dy in (1, 2, 3):
-        tap_y(dy, my_y).start()
-
+    taps_to_y()
     seg_wait(OM0, so.at[0], ro.at[0])
     seg_wait(OM1, so.at[1], ro.at[1])
     seg_wait(OL, sol, rol)
+    taps_to_z()
     home(ro, rol, out_ref)
-    for dy in (1, 2, 3):
-        tap_y(dy, (my_y + 4 - dy) % 4).wait_recv()
-    dkz[my_z] = (dky[0] + dky[1]) + (dky[2] + dky[3])
-    for dz in (1, 2, 3):
-        tap_z(dz, my_z).start()
+    taps_back_y()
     point_end()
+    taps_back_pair()
     seg_wait(IM0, si.at[0], ri.at[0])
     seg_wait(IM1, si.at[1], ri.at[1])
     seg_wait(IL, sil, ril)
     home(ri, ril, gin_ref)
-    for dz in (1, 2, 3):
-        tap_z(dz, (my_z + 4 - dz) % 4).wait_recv()
-    dgrad_ref[...] = ((dkz[0] + dkz[1]) + (dkz[2] + dkz[3]))[:25]
+    taps_end()
 
     for j in range(2):
         seg_sent((XM0, XM1)[j], sx.at[j], rx.at[j])
@@ -480,31 +540,16 @@
     for y in range(4):
         pair_copy(y).wait_send()
     tap_pair().wait_send()
+    tap_back_pair(core).wait_send()
     for d in (1, 2, 3):
         y_copy(d).wait_send()
         z_copy(d).wait_send()
-        tap_y(d, my_y).wait_send()
+        tap_y(d).wait_send()
         tap_z(d, my_z).wait_send()
-
-
-def tap_mask(op_kind):
-    tap_index = jnp.arange(25, dtype=jnp.int32)
-    row_shift = tap_index // 5 - 2
-    col_shift = tap_index % 5 - 2
-    narrow = (jnp.abs(row_shift) <= 1) & (jnp.abs(col_shift) <= 1)
-    spaced = (row_shift % 2 == 0) & (col_shift % 2 == 0)
-    tap_keep = jnp.where(op_kind == 0, narrow, jnp.where(op_kind == 1, True, spaced))
-    return tap_keep.astype(jnp.float32)
+        tap_back_y(d, my_y).wait_send()
 
 
 def body(feature_maps, path_lists, point_weight, depth_kernel, cotangent):
-    section = lax.axis_index("segment")
-    path = path_lists[0, :, 0]
-    index = jnp.arange(8, dtype=jnp.int32)
-    same = (path[None, :] == path[:, None]) & (index[None, :] < index[:, None])
-    slot = path * 2 + jnp.sum(same.astype(jnp.int32), axis=1)
-    slots = jnp.tile(slot, 16)[None, :]
-    keep = tap_mask(section % 3)[:, None]
     x = feature_maps.transpose(1, 2, 0, 3).reshape(POS * 8, C)
     g = cotangent.transpose(1, 2, 0, 3).reshape(POS * 8, C)
     vmem = pl.BlockSpec(memory_space=pltpu.VMEM)
@@ -518,9 +563,9 @@
             jax.ShapeDtypeStruct((POS * 8, C), BF16),
             jax.ShapeDtypeStruct((POS * 8, C), BF16),
             jax.ShapeDtypeStruct((32, C), F32),
-            jax.ShapeDtypeStruct((25, C), F32),
+            jax.ShapeDtypeStruct((25, 1, C), F32),
         ),
-        in_specs=[vmem] * 5,
+        in_specs=[pl.BlockSpec(memory_space=pltpu.SMEM)] + [vmem] * 4,
         out_specs=[vmem] * 4,
         scratch_shapes=[
             *[main, main, last, last] * 4,
@@ -536,23 +581,25 @@
             pltpu.VMEM((3, 32, C), BF16),
             pltpu.VMEM((3, 32, C), BF16),
             pltpu.VMEM((25, 8, C), F32),
-            pltpu.VMEM((2, 32, C), F32),
-            pltpu.VMEM((4, 32, C), F32),
-            pltpu.VMEM((4, 32, C), F32),
+            pltpu.VMEM((2, 4, 32, LANES), F32),
+            pltpu.VMEM((4, 32, LANES), F32),
+            pltpu.VMEM((3, 32, LANES), F32),
+            pltpu.VMEM((4, 32, LANES), F32),
+            pltpu.VMEM((2, 4, 32, LANES), F32),
             pltpu.SemaphoreType.DMA((12, SEG)),
             pltpu.SemaphoreType.DMA((12, SEG)),
             pltpu.SemaphoreType.DMA((12,)),
-            pltpu.SemaphoreType.DMA((17,)),
-            pltpu.SemaphoreType.DMA((17,)),
+            pltpu.SemaphoreType.DMA((21,)),
+            pltpu.SemaphoreType.DMA((21,)),
         ],
         compiler_params=pltpu.CompilerParams(
             collective_id=0, has_side_effects=True, vmem_limit_bytes=60 * 1024 * 1024
         ),
         name="supernet_window",
-    )(slots, x, g, point_weight[0, 0], depth_kernel[0, 0] * keep)
+    )(path_lists[:, :, 0], x, g, point_weight[0, 0], depth_kernel[0].reshape(25, 1, C))
     final = out.reshape(SIDE, SIDE, 8, C).transpose(2, 0, 1, 3)
     grad = gin.reshape(SIDE, SIDE, 8, C).transpose(2, 0, 1, 3)
-    return final, grad, pgrad[None, None], (dgrad * keep)[None, None]
+    return final, grad, pgrad[None, None], dgrad.reshape(1, 1, 25, C)
 
 
 def solution(mesh):

time: 111 us -> 105 us (0.946)
  other arithmetic: 4.28 us -> 0 us
    mul x1 -> x0, other arithmetic: 1.63 us -> none  [body(): depth_kernel[0, 0] * keep]
    unnamed x8 -> x10, local copies, waits for them, and re-layouts: 4.37 us -> 4.35 us
where the time goes in v2:
time: 105 us; the launch traced here: 104 us
  Pallas kernels  99.4 us (95%)
  local copies, waits for them, and re-layouts  4.35 us (4%)
    pallas_call x1, Pallas kernels, body(): pl.pallas_call(kernel, out_shape=(jax.ShapeDtypeStruct((POS * 8, C), BF16...  99.4 us
    unnamed x10, local copies, waits for them, and re-layouts  4.35 us

profile of v2, /device:TPU:1, one launch (start us, length us, event | category | flops | bytes accessed | tf_op | source)
XLA Modules:
  0.0 104.4 jit_solution(13390979263841841039)
XLA Ops:
  0.6 99.4 %supernet_window.1 = (bf16[392,1024]{1,0:T(8,128)(2,1)}, bf16[392,1024]{1,0:T(8,128)(2,1)}, f32[32,1024]{1,0:T(8,128)}, f32[25,1,1024]{2,1,0:T(1,128)}) custom-call(s32[1,8]{1,0:T(1,128)} %bitcast.27, bf16[392,1024]{1,0:T(8,128)(2,1)} %bitcast.20, bf16[392,1024]{1,0:T(8,128)(2,1)} %bitcast.21, bf16[1024,1024]{1,0:T(8,128)(2,1)} %bitcast.19, ...), custom_call_target="tpu_custom_call" | custom-call | tf_op jit(solution)/shard_map/supernet_window/pallas_call | solution.py:560
  100.0 0.0 copy-start
  100.0 0.0 copy-start.1
  100.0 0.0 copy-start.2
  100.0 2.2 %copy.14 = bf16[8,7,7,1024]{3,0,2,1:T(8,128)(2,1)} copy(bf16[8,7,7,1024]{3,0,2,1:T(8,128)(2,1)} %bitcast.23) | data formatting | bytes 1605632
  102.2 0.0 copy-done
  102.2 0.9 copy.15
  103.1 0.0 copy-done.1
  103.1 0.7 copy.16
  103.8 0.0 copy-done.2
  103.8 0.6 copy.17
Async XLA Ops:
  100.0 2.2 %copy-start = (bf16[392,1024]{1,0:T(8,128)(2,1)S(1)}, bf16[392,1024]{1,0:T(8,128)(2,1)}, u32[]{:S(2)}) copy-start(bf16[392,1024]{1,0:T(8,128)(2,1)} %get-tuple-element.9) | copy-start | bytes 2408452
  100.0 3.1 %copy-start.1 = (f32[32,1024]{1,0:T(8,128)S(1)}, f32[32,1024]{1,0:T(8,128)}, u32[]{:S(2)}) copy-start(f32[32,1024]{1,0:T(8,128)} %get-tuple-element.10) | copy-start | bytes 393220
  100.0 3.7 %copy-start.2 = (f32[25,1,1024]{2,1,0:T(1,128)S(1)}, f32[25,1,1024]{2,1,0:T(1,128)}, u32[]{:S(2)}) copy-start(f32[25,1,1024]{2,1,0:T(1,128)} %get-tuple-element.11) | copy-start | bytes 307204

commit v3 on v2

--- a/solution.py
+++ b/solution.py
@@ -41,14 +41,15 @@
 
 def kernel(
     path_ref,
-    x_ref,
-    g_ref,
-    w_ref,
-    k_ref,
-    out_ref,
-    gin_ref,
+    x_in,
+    g_in,
+    w_in,
+    k_in,
+    out_hbm,
+    gin_hbm,
     pgrad_ref,
     dgrad_ref,
+    x_ref, g_ref, w_ref, k_ref, out_ref, gin_ref,
     sx, rx, sxl, rxl,
     sg, rg, sgl, rgl,
     so, ro, sol, rol,
@@ -57,56 +58,71 @@
     fold_o, fold_i,
     pg, prx, psb, prb, psc, prc,
     dka, tap_own, tap_pair_in, tap_y_in, tap_z_all, tap_all,
-    send_sem, recv_sem, local_sem, rsend, rrecv,
+    send_sem, recv_sem, local_sem, rsend, rrecv, load_sem,
 ):
     me = lax.axis_index("segment")
     rep = lax.axis_index("rep")
-    z_lo = me // 4
-    xx = me % 4
-    my_y = rep // 8
-    my_z = (rep // 2) % 4
-    core = rep % 2
+    z_lo = me >> 2
+    xx = me & 3
+    my_y = rep >> 3
+    my_z = (rep >> 1) & 3
+    core = rep & 1
+
+    def rep_at(dy, dz, dc):
+        return (((my_y + dy) & 3) << 3) + (((my_z + dz) & 3) << 1) + ((core + dc) & 1)
+
+    outside = rep_at(0, 2 * z_lo - 1, 0)
 
     def seg_at(dz, dx):
-        return ((z_lo + dz) % 2) * 4 + (xx + dx) % 4
-
-    def rep_at(dy, dz, dc):
-        return ((my_y + dy) % 4) * 8 + ((my_z + dz) % 4) * 2 + (core + dc) % 2
+        return (((z_lo + dz) & 1) << 2) + ((xx + dx) & 3)
+
+    def seg_device(dz, dx):
+        return (seg_at(dz, dx), outside if dz and dx & 1 else rep)
 
     rep_partners = ((0, 0, 1), (1, 0, 0), (2, 0, 0), (3, 0, 0), (0, 1, 0), (0, 2, 0), (0, 3, 0))
 
     barrier = pltpu.get_barrier_semaphore()
-    for dz, dx in PARTNERS:
-        pl.semaphore_signal(barrier, inc=1, device_id=(seg_at(dz, dx), rep), device_id_type=MESH)
     for dy, dz, dc in rep_partners:
         pl.semaphore_signal(
             barrier, inc=1, device_id=(me, rep_at(dy, dz, dc)), device_id_type=MESH
         )
-
-    def seg_copy(kind, src, dst, there, slot):
+    for dz, dx in PARTNERS:
+        pl.semaphore_signal(barrier, inc=1, device_id=seg_device(dz, dx), device_id_type=MESH)
+
+    loads = [
+        pltpu.make_async_copy(far, near, load_sem.at[i])
+        for i, (far, near) in enumerate(
+            ((x_in, x_ref), (g_in, g_ref), (k_in, k_ref), (w_in, w_ref))
+        )
+    ]
+    for load in loads:
+        load.start()
+
+    def seg_copy(kind, src, dst, dz, dx, received=False):
+        there = seg_at(dz, dx)
+        slot = there if received else me
         return pltpu.make_async_remote_copy(
             src_ref=src.at[there],
             dst_ref=dst.at[slot],
             send_sem=send_sem.at[kind, there],
             recv_sem=recv_sem.at[kind, slot],
-            device_id=(there, rep),
+            device_id=seg_device(dz, dx),
             device_id_type=MESH,
         )
 
     def seg_send(kind, src, dst):
         for dz, dx in PARTNERS:
-            seg_copy(kind, src, dst, seg_at(dz, dx), me).start()
+            seg_copy(kind, src, dst, dz, dx).start()
         pltpu.make_async_copy(src.at[me], dst.at[me], local_sem.at[kind]).start()
 
     def seg_wait(kind, src, dst):
         pltpu.make_async_copy(src.at[me], dst.at[me], local_sem.at[kind]).wait()
         for dz, dx in PARTNERS:
-            there = seg_at(dz, dx)
-            seg_copy(kind, src, dst, there, there).wait_recv()
+            seg_copy(kind, src, dst, dz, dx, received=True).wait_recv()
 
     def seg_sent(kind, src, dst):
         for dz, dx in PARTNERS:
-            seg_copy(kind, src, dst, seg_at(dz, dx), me).wait_send()
+            seg_copy(kind, src, dst, dz, dx).wait_send()
 
     paths = [path_ref[0, i] for i in range(8)]
     slot_of = []
@@ -159,16 +175,19 @@
         ).astype(BF16)
         last[...] = mm(route_last, folded).astype(BF16).reshape(8, 16, LANES)
 
+    loads[0].wait()
     dispatch(x_ref, sx, sxl)
     pl.semaphore_wait(barrier, 14)
     seg_send(XM0, sx.at[0], rx.at[0])
     seg_send(XL, sxl, rxl)
+    loads[1].wait()
     dispatch(g_ref, sg, sgl)
     seg_send(GM0, sg.at[0], rg.at[0])
     seg_send(GL, sgl, rgl)
     seg_send(XM1, sx.at[1], rx.at[1])
     seg_send(GM1, sg.at[1], rg.at[1])
 
+    loads[2].wait()
     kind = me % 3
     keep = []
     for t in range(25):
@@ -380,14 +399,14 @@
             device_id_type=MESH,
         )
 
-    sibling = (core + 1) % 2
+    sibling = 1 - core
 
     def pair_copy(y):
         return rep_copy(y, pg.at[y, :, sibling], prx.at[y], 0, 0, 1)
 
     def point_terms(j):
         for dy in (1, 2, 3, 0):
-            y = (my_y + dy) % 4
+            y = (my_y + dy) & 3
             cols = pl.ds(pl.multiple_of(y * 256, 256), 256)
             for part in range(4):
                 lanes = slice(part * 256, part * 256 + 256)
@@ -412,7 +431,7 @@
 
     def point_over_y():
         for dy in (1, 2, 3, 0):
-            y = (my_y + dy) % 4
+            y = (my_y + dy) & 3
             pair_copy(y).wait_recv()
             total = pg[y, :, core] + prx[y]
             if dy:
@@ -429,7 +448,7 @@
             total = total + prb[slot].astype(F32)
         prx[my_y] = total
         for dz in (1, 2, 3):
-            psc[dz - 1] = prx[my_y, (my_z + dz) % 4].astype(BF16)
+            psc[dz - 1] = prx[my_y, (my_z + dz) & 3].astype(BF16)
             z_copy(dz).start()
 
     def point_end():
@@ -444,7 +463,7 @@
         return rep_copy(10, tap_own.at[sibling], tap_pair_in, 0, 0, 1)
 
     def tap_y(dy):
-        return rep_copy(10 + dy, tap_own.at[core, (my_y + dy) % 4], tap_y_in.at[dy - 1], dy, 0, 0)
+        return rep_copy(10 + dy, tap_own.at[core, (my_y + dy) & 3], tap_y_in.at[dy - 1], dy, 0, 0)
 
     def tap_z(dz, slot):
         return rep_copy(13 + dz, tap_z_all.at[my_z], tap_z_all.at[slot], 0, dz, 0)
@@ -458,7 +477,7 @@
     def taps_to_pair():
         sums = jnp.concatenate([jnp.sum(dka[...], axis=1), jnp.zeros((7, C), F32)], axis=0)
         for block in range(8):
-            tap_own[block // 4, block % 4] = sums[:, block * LANES : block * LANES + LANES]
+            tap_own[block // 4, block & 3] = sums[:, block * LANES : block * LANES + LANES]
         tap_pair().start()
 
     def taps_to_y():
@@ -478,22 +497,23 @@
 
     def taps_back_y():
         for dz in (1, 2, 3):
-            tap_z(dz, (my_z + 4 - dz) % 4).wait_recv()
+            tap_z(dz, (my_z + 4 - dz) & 3).wait_recv()
         tap_all[core, my_y] = (tap_z_all[0] + tap_z_all[1]) + (tap_z_all[2] + tap_z_all[3])
         for dy in (1, 2, 3):
             tap_back_y(dy, my_y).start()
 
     def taps_back_pair():
         for dy in (1, 2, 3):
-            tap_back_y(dy, (my_y + 4 - dy) % 4).wait_recv()
+            tap_back_y(dy, (my_y + 4 - dy) & 3).wait_recv()
         tap_back_pair(core).start()
 
     def taps_end():
         tap_back_pair(sibling).wait_recv()
-        sums = jnp.concatenate([tap_all[b // 4, b % 4] for b in range(8)], axis=1)
+        sums = jnp.concatenate([tap_all[b // 4, b & 3] for b in range(8)], axis=1)
         for t in range(25):
             dgrad_ref[t] = sums[t : t + 1] * keep[t]
 
+    loads[3].wait()
     forward(0)
     receive_g(0)
     backward(0)
@@ -519,6 +539,8 @@
     seg_wait(OL, sol, rol)
     taps_to_z()
     home(ro, rol, out_ref)
+    store_out = pltpu.make_async_copy(out_ref, out_hbm, load_sem.at[4])
+    store_out.start()
     taps_back_y()
     point_end()
     taps_back_pair()
@@ -526,6 +548,8 @@
     seg_wait(IM1, si.at[1], ri.at[1])
     seg_wait(IL, sil, ril)
     home(ri, ril, gin_ref)
+    store_gin = pltpu.make_async_copy(gin_ref, gin_hbm, load_sem.at[5])
+    store_gin.start()
     taps_end()
 
     for j in range(2):
@@ -547,12 +571,16 @@
         tap_y(d).wait_send()
         tap_z(d, my_z).wait_send()
         tap_back_y(d, my_y).wait_send()
+    store_out.wait()
+    store_gin.wait()
 
 
 def body(feature_maps, path_lists, point_weight, depth_kernel, cotangent):
     x = feature_maps.transpose(1, 2, 0, 3).reshape(POS * 8, C)
     g = cotangent.transpose(1, 2, 0, 3).reshape(POS * 8, C)
     vmem = pl.BlockSpec(memory_space=pltpu.VMEM)
+    anywhere = pl.BlockSpec(memory_space=pl.ANY)
+    maps = pltpu.VMEM((POS * 8, C), BF16)
     main = pltpu.VMEM((2, SEG, MAIN, C), BF16)
     last = pltpu.VMEM((SEG, 16, LANES), BF16)
     wide = pltpu.VMEM((2, ROWS, C), F32)
@@ -565,9 +593,10 @@
             jax.ShapeDtypeStruct((32, C), F32),
             jax.ShapeDtypeStruct((25, 1, C), F32),
         ),
-        in_specs=[pl.BlockSpec(memory_space=pltpu.SMEM)] + [vmem] * 4,
-        out_specs=[vmem] * 4,
+        in_specs=[pl.BlockSpec(memory_space=pltpu.SMEM)] + [anywhere] * 4,
+        out_specs=[anywhere] * 2 + [vmem] * 2,
         scratch_shapes=[
+            maps, maps, pltpu.VMEM((C, C), BF16), pltpu.VMEM((25, 1, C), F32), maps, maps,
             *[main, main, last, last] * 4,
             wide, wide, wide, wide, narrow, narrow,
             pltpu.VMEM((2, ROWS, LANES), F32),
@@ -591,6 +620,7 @@
             pltpu.SemaphoreType.DMA((12,)),
             pltpu.SemaphoreType.DMA((21,)),
             pltpu.SemaphoreType.DMA((21,)),
+            pltpu.SemaphoreType.DMA((6,)),
         ],
         compiler_params=pltpu.CompilerParams(
             collective_id=0, has_side_effects=True, vmem_limit_bytes=60 * 1024 * 1024

time: 105 us -> 98.2 us (0.935)
  Pallas kernels: 99.4 us -> 93 us
    pallas_call x1, Pallas kernels: 99.4 us -> 93 us  [body(): pl.pallas_call(kernel, out_shape=(jax.ShapeDtypeStruct((POS * 8, C), BF16...]
where the time goes in v3:
time: 98.2 us; the launch traced here: 98.1 us
  Pallas kernels  93 us (95%)
  local copies, waits for them, and re-layouts  4.35 us (4%)
    pallas_call x1, Pallas kernels, body(): pl.pallas_call(kernel, out_shape=(jax.ShapeDtypeStruct((POS * 8, C), BF16...  93 us
    unnamed x10, local copies, waits for them, and re-layouts  4.35 us

profile of v3, /device:TPU:1, one launch (start us, length us, event | category | flops | bytes accessed | tf_op | source)
XLA Modules:
  0.0 98.1 jit_solution(8051352010567292579)
XLA Ops:
  0.6 93.0 %supernet_window.1 = (bf16[392,1024]{1,0:T(8,128)(2,1)}, bf16[392,1024]{1,0:T(8,128)(2,1)}, f32[32,1024]{1,0:T(8,128)}, f32[25,1,1024]{2,1,0:T(1,128)}) custom-call(s32[1,8]{1,0:T(1,128)} %bitcast.27, bf16[392,1024]{1,0:T(8,128)(2,1)} %bitcast.20, bf16[392,1024]{1,0:T(8,128)(2,1)} %bitcast.21, bf16[1024,1024]{1,0:T(8,128)(2,1)} %bitcast.19, ...), custom_call_target="tpu_custom_call" | custom-call | tf_op jit(solution)/shard_map/supernet_window/pallas_call | solution.py:588
  93.7 0.0 copy-start
  93.7 0.0 copy-start.1
  93.7 0.0 copy-start.2
  93.7 2.2 %copy.14 = bf16[8,7,7,1024]{3,0,2,1:T(8,128)(2,1)} copy(bf16[8,7,7,1024]{3,0,2,1:T(8,128)(2,1)} %bitcast.23) | data formatting | bytes 1605632
  95.9 0.0 copy-done
  95.9 0.9 copy.15
  96.8 0.0 copy-done.1
  96.8 0.7 copy.16
  97.4 0.0 copy-done.2
  97.4 0.6 copy.17
Async XLA Ops:
  93.7 2.2 %copy-start = (bf16[392,1024]{1,0:T(8,128)(2,1)S(1)}, bf16[392,1024]{1,0:T(8,128)(2,1)}, u32[]{:S(2)}) copy-start(bf16[392,1024]{1,0:T(8,128)(2,1)} %get-tuple-element.9) | copy-start | bytes 2408452
  93.7 3.1 %copy-start.1 = (f32[32,1024]{1,0:T(8,128)S(1)}, f32[32,1024]{1,0:T(8,128)}, u32[]{:S(2)}) copy-start(f32[32,1024]{1,0:T(8,128)} %get-tuple-element.10) | copy-start | bytes 393220
  93.7 3.7 %copy-start.2 = (f32[25,1,1024]{2,1,0:T(1,128)S(1)}, f32[25,1,1024]{2,1,0:T(1,128)}, u32[]{:S(2)}) copy-start(f32[25,1,1024]{2,1,0:T(1,128)} %get-tuple-element.11) | copy-start | bytes 307204

commit v4 on v3

--- a/solution.py
+++ b/solution.py
@@ -19,7 +19,7 @@
 ROWS = 400
 LANES = 128
 SEG = 8
-PARTNERS = ((1, 0), (0, 1), (0, 3), (1, 1), (1, 3), (0, 2), (1, 2))
+PARTNERS = ((0, 2), (1, 2), (0, 1), (0, 3), (1, 1), (1, 3), (1, 0))
 
 XM0, XM1, XL, GM0, GM1, GL, OM0, OM1, OL, IM0, IM1, IL = range(12)
 
@@ -544,6 +544,22 @@
     taps_back_y()
     point_end()
     taps_back_pair()
+    for j in range(2):
+        seg_sent((XM0, XM1)[j], sx.at[j], rx.at[j])
+        seg_sent((GM0, GM1)[j], sg.at[j], rg.at[j])
+        seg_sent((OM0, OM1)[j], so.at[j], ro.at[j])
+    seg_sent(IM0, si.at[0], ri.at[0])
+    seg_sent(XL, sxl, rxl)
+    seg_sent(GL, sgl, rgl)
+    seg_sent(OL, sol, rol)
+    for y in range(4):
+        pair_copy(y).wait_send()
+    tap_pair().wait_send()
+    for d in (1, 2, 3):
+        y_copy(d).wait_send()
+        z_copy(d).wait_send()
+        tap_y(d).wait_send()
+        tap_z(d, my_z).wait_send()
     seg_wait(IM0, si.at[0], ri.at[0])
     seg_wait(IM1, si.at[1], ri.at[1])
     seg_wait(IL, sil, ril)
@@ -552,24 +568,10 @@
     store_gin.start()
     taps_end()
 
-    for j in range(2):
-        seg_sent((XM0, XM1)[j], sx.at[j], rx.at[j])
-        seg_sent((GM0, GM1)[j], sg.at[j], rg.at[j])
-        seg_sent((OM0, OM1)[j], so.at[j], ro.at[j])
-        seg_sent((IM0, IM1)[j], si.at[j], ri.at[j])
-    seg_sent(XL, sxl, rxl)
-    seg_sent(GL, sgl, rgl)
-    seg_sent(OL, sol, rol)
+    seg_sent(IM1, si.at[1], ri.at[1])
     seg_sent(IL, sil, ril)
-    for y in range(4):
-        pair_copy(y).wait_send()
-    tap_pair().wait_send()
     tap_back_pair(core).wait_send()
     for d in (1, 2, 3):
-        y_copy(d).wait_send()
-        z_copy(d).wait_send()
-        tap_y(d).wait_send()
-        tap_z(d, my_z).wait_send()
         tap_back_y(d, my_y).wait_send()
     store_out.wait()
     store_gin.wait()

time: 98.2 us -> 97.5 us (level)
  no operation moved by 1% of the time
where the time goes in v4:
time: 97.5 us; the launch traced here: 97.4 us
  Pallas kernels  92.4 us (95%)
  local copies, waits for them, and re-layouts  4.35 us (4%)
    pallas_call x1, Pallas kernels, body(): pl.pallas_call(kernel, out_shape=(jax.ShapeDtypeStruct((POS * 8, C), BF16...  92.4 us
    unnamed x10, local copies, waits for them, and re-layouts  4.35 us

profile of v4, /device:TPU:1, one launch (start us, length us, event | category | flops | bytes accessed | tf_op | source)
XLA Modules:
  0.0 97.4 jit_solution(16795232797778600488)
XLA Ops:
  0.6 92.4 %supernet_window.1 = (bf16[392,1024]{1,0:T(8,128)(2,1)}, bf16[392,1024]{1,0:T(8,128)(2,1)}, f32[32,1024]{1,0:T(8,128)}, f32[25,1,1024]{2,1,0:T(1,128)}) custom-call(s32[1,8]{1,0:T(1,128)} %bitcast.27, bf16[392,1024]{1,0:T(8,128)(2,1)} %bitcast.20, bf16[392,1024]{1,0:T(8,128)(2,1)} %bitcast.21, bf16[1024,1024]{1,0:T(8,128)(2,1)} %bitcast.19, ...), custom_call_target="tpu_custom_call" | custom-call | tf_op jit(solution)/shard_map/supernet_window/pallas_call | solution.py:590
  93.0 0.0 copy-start
  93.0 0.0 copy-start.1
  93.1 0.0 copy-start.2
  93.1 2.2 %copy.14 = bf16[8,7,7,1024]{3,0,2,1:T(8,128)(2,1)} copy(bf16[8,7,7,1024]{3,0,2,1:T(8,128)(2,1)} %bitcast.23) | data formatting | bytes 1605632
  95.2 0.0 copy-done
  95.2 0.9 copy.15
  96.1 0.0 copy-done.1
  96.1 0.7 copy.16
  96.8 0.0 copy-done.2
  96.8 0.6 copy.17
Async XLA Ops:
  93.0 2.2 %copy-start = (bf16[392,1024]{1,0:T(8,128)(2,1)S(1)}, bf16[392,1024]{1,0:T(8,128)(2,1)}, u32[]{:S(2)}) copy-start(bf16[392,1024]{1,0:T(8,128)(2,1)} %get-tuple-element.9) | copy-start | bytes 2408452
  93.0 3.1 %copy-start.1 = (f32[32,1024]{1,0:T(8,128)S(1)}, f32[32,1024]{1,0:T(8,128)}, u32[]{:S(2)}) copy-start(f32[32,1024]{1,0:T(8,128)} %get-tuple-element.10) | copy-start | bytes 393220
  93.1 3.7 %copy-start.2 = (f32[25,1,1024]{2,1,0:T(1,128)S(1)}, f32[25,1,1024]{2,1,0:T(1,128)}, u32[]{:S(2)}) copy-start(f32[25,1,1024]{2,1,0:T(1,128)} %get-tuple-element.11) | copy-start | bytes 307204

commit v5 on v4

--- a/solution.py
+++ b/solution.py
@@ -524,9 +524,9 @@
     point_terms(1)
     back_project(1)
     back_activate(1)
-    point_over_y()
     convolve(1, gh32, -1, emit_gin)
     send_gin(1)
+    point_over_y()
     seg_send(IM1, si.at[1], ri.at[1])
     send_last(fold_i, sil)
     seg_send(IL, sil, ril)

time: 97.5 us -> 100 us (1.026)
  Pallas kernels: 92.4 us -> 95.3 us
    pallas_call x1, Pallas kernels: 92.4 us -> 95.3 us  [body(): pl.pallas_call(kernel, out_shape=(jax.ShapeDtypeStruct((POS * 8, C), BF16...]
where the time goes in v5:
time: 100 us
  Pallas kernels  95.3 us (95%)
  local copies, waits for them, and re-layouts  4.35 us (4%)
    pallas_call x1, Pallas kernels, body(): pl.pallas_call(kernel, out_shape=(jax.ShapeDtypeStruct((POS * 8, C), BF16...  95.3 us
    unnamed x10, local copies, waits for them, and re-layouts  4.35 us

profile of v5, /device:TPU:1, one launch (start us, length us, event | category | flops | bytes accessed | tf_op | source)
XLA Modules:
  0.0 100.3 jit_solution(14323621171332030710)
XLA Ops:
  0.6 95.3 %supernet_window.1 = (bf16[392,1024]{1,0:T(8,128)(2,1)}, bf16[392,1024]{1,0:T(8,128)(2,1)}, f32[32,1024]{1,0:T(8,128)}, f32[25,1,1024]{2,1,0:T(1,128)}) custom-call(s32[1,8]{1,0:T(1,128)} %bitcast.27, bf16[392,1024]{1,0:T(8,128)(2,1)} %bitcast.20, bf16[392,1024]{1,0:T(8,128)(2,1)} %bitcast.21, bf16[1024,1024]{1,0:T(8,128)(2,1)} %bitcast.19, ...), custom_call_target="tpu_custom_call" | custom-call | tf_op jit(solution)/shard_map/supernet_window/pallas_call | solution.py:590
  95.9 0.0 copy-start
  95.9 0.0 copy-start.1
  95.9 0.0 copy-start.2
  95.9 2.2 %copy.14 = bf16[8,7,7,1024]{3,0,2,1:T(8,128)(2,1)} copy(bf16[8,7,7,1024]{3,0,2,1:T(8,128)(2,1)} %bitcast.23) | data formatting | bytes 1605632
  98.1 0.0 copy-done
  98.1 0.9 copy.15
  99.0 0.0 copy-done.1
  99.0 0.7 copy.16
  99.6 0.0 copy-done.2
  99.6 0.6 copy.17
Async XLA Ops:
  95.9 2.2 %copy-start = (bf16[392,1024]{1,0:T(8,128)(2,1)S(1)}, bf16[392,1024]{1,0:T(8,128)(2,1)}, u32[]{:S(2)}) copy-start(bf16[392,1024]{1,0:T(8,128)(2,1)} %get-tuple-element.9) | copy-start | bytes 2408452
  95.9 3.1 %copy-start.1 = (f32[32,1024]{1,0:T(8,128)S(1)}, f32[32,1024]{1,0:T(8,128)}, u32[]{:S(2)}) copy-start(f32[32,1024]{1,0:T(8,128)} %get-tuple-element.10) | copy-start | bytes 393220
  95.9 3.7 %copy-start.2 = (f32[25,1,1024]{2,1,0:T(1,128)S(1)}, f32[25,1,1024]{2,1,0:T(1,128)}, u32[]{:S(2)}) copy-start(f32[25,1,1024]{2,1,0:T(1,128)} %get-tuple-element.11) | copy-start | bytes 307204
